TPU v7x, 32 devices: a whole 2x2x4 slice. The times are simulated.
32 devices in a mesh: slab: 4 (over y, core), hst: 8 (over z, x).
Axes of the slice: x: 2, y: 2, z: 4, core: 2. Of those that a mesh axis runs over, the one named last changes fastest.
Arguments:
- load: bfloat16 [288, 65536], P('slab', 'hst'), may hold values from -6 to 6
- host_rack: int32 [65536], P('hst'), may hold values from 0 to 2047, as said below
- rack_pod: int32 [2048], P('hst'), may hold values from 0 to 15
Outputs:
- host_drift: float32 [288, 65536], P('slab', 'hst')
- rack_drift: float32 [288, 2048], P('slab', 'hst')
- pod_drift: float32 [288, 16], P('slab', 'hst')
Inputs may be any that keep to these rules, and one draw needn't show every extreme that they name: `host_rack`: the hosts s * 8192 to (s + 1) * 8192 - 1 belong to racks among s * 256 to (s + 2) * 256 - 1, counted modulo 2048; racks hold uneven numbers of hosts, some none.
All inputs are finite; a program needn't handle non-finite values.
Results may differ from a plain program's by a relative error of at most 0.0003.
Values may be sent and summed in bfloat16 or wider, within the bound.
A program may use at most 64 MiB of HBM per device.

v0:
```python
import math

import jax
import jax.numpy as jnp
from jax import lax
from jax.sharding import PartitionSpec as P

SLAB_LEN = 36
POD_DEV = 2


def carried_in(part, axis, combine, identity):
    place = lax.axis_index(axis)
    gathered = lax.all_gather(part, axis)
    state = jnp.zeros_like(part) + jnp.asarray(identity, part.dtype)

    def one(hop, state):
        return combine(state, lax.dynamic_index_in_dim(gathered, hop, 0, False))

    return lax.fori_loop(0, place, one, state)


def passed_along(value, axis, steps):
    count = lax.axis_size(axis)
    pairs = [(source, (source + steps) % count) for source in range(count)]
    return lax.ppermute(value, axis, pairs)


def with_halo(cells, sides, width):
    for axis, dim in sides:
        count = lax.axis_size(axis)
        head = lax.slice_in_dim(cells, 0, width, axis=dim)
        tail = lax.slice_in_dim(cells, cells.shape[dim] - width, cells.shape[dim], axis=dim)
        cells = jnp.concatenate(
            [
                lax.ppermute(tail, axis, [(i, (i + 1) % count) for i in range(count)]),
                cells,
                lax.ppermute(head, axis, [((i + 1) % count, i) for i in range(count)]),
            ],
            axis=dim,
        )
    return cells


def band_ones(step_rows, reach_steps, dtype):
    row_ids = lax.broadcasted_iota(jnp.int32, (step_rows, 3 * step_rows), 0)
    col_ids = lax.broadcasted_iota(jnp.int32, (step_rows, 3 * step_rows), 1)
    return (jnp.abs(col_ids - row_ids - step_rows) <= reach_steps).astype(dtype)


def lower_ones(step_rows):
    row_ids = lax.broadcasted_iota(jnp.int32, (step_rows, step_rows), 0)
    col_ids = lax.broadcasted_iota(jnp.int32, (step_rows, step_rows), 1)
    return (col_ids <= row_ids).astype(jnp.float32)


def local_prefix(series, extended, band, lower, window_size, precision):
    window_sums = jnp.dot(band, extended, preferred_element_type=jnp.float32, precision=precision)
    deviation = series.astype(jnp.float32) - window_sums / window_size
    return jnp.dot(
        lower, deviation, preferred_element_type=jnp.float32, precision=lax.Precision.HIGHEST
    )


def add_pair(earlier, later):
    return earlier + later


def slab_carry(totals):
    return carried_in(totals, "slab", add_pair, jnp.zeros_like(totals))


def rack_and_pod(series, local_rack, rack_pod):
    rack_count = rack_pod.shape[0]
    columns = lax.broadcasted_iota(jnp.int32, (1, 2 * rack_count), 1)
    member = (local_rack[:, None] == columns).astype(series.dtype)
    partial_sums = jnp.dot(series, member, preferred_element_type=jnp.float32, precision=None)
    arrived = passed_along(partial_sums[:, rack_count:], "hst", 1)
    rack_totals = partial_sums[:, :rack_count] + arrived
    pod_total = POD_DEV * lax.axis_size("hst")
    pod_columns = lax.broadcasted_iota(jnp.int32, (1, pod_total), 1)
    pod_member = (rack_pod[:, None] == pod_columns).astype(jnp.float32)
    pod_terms = jnp.dot(
        rack_totals, pod_member, preferred_element_type=jnp.float32, precision=lax.Precision.HIGHEST
    )
    pod_totals = lax.psum_scatter(pod_terms, "hst", scatter_dimension=1, tiled=True)
    return (rack_totals, pod_totals)


def on_device(load, host_rack, rack_pod):
    step_rows, hosts_here = load.shape
    rack_count = rack_pod.shape[0]
    total_racks = rack_count * lax.axis_size("hst")
    local_rack = (host_rack - lax.axis_index("hst") * rack_count) % total_racks
    reach_steps = 2 * SLAB_LEN
    window_size = 2 * reach_steps + 1
    day_steps = step_rows * lax.axis_size("slab")
    lower = lower_ones(step_rows)
    extended = with_halo(load, (("slab", 0),), step_rows)
    host_prefix = local_prefix(
        load, extended, band_ones(step_rows, reach_steps, jnp.bfloat16), lower, window_size, None
    )
    rack_load, pod_load = rack_and_pod(load, local_rack, rack_pod)
    groups = jnp.concatenate([rack_load, pod_load], 1)
    group_ext = with_halo(groups, (("slab", 0),), step_rows)
    group_prefix = local_prefix(
        groups,
        group_ext,
        band_ones(step_rows, reach_steps, jnp.float32),
        lower,
        window_size,
        lax.Precision.HIGHEST,
    )
    carried = slab_carry(jnp.concatenate([host_prefix[-1], group_prefix[-1]], 0))
    host_sum = host_prefix + carried[None, :hosts_here]
    group_sum = group_prefix + carried[None, hosts_here:]
    rack_sum = group_sum[:, :rack_count]
    pod_sum = group_sum[:, rack_count:]
    host_drift = host_sum * (1.0 / math.sqrt(day_steps))
    rack_drift = rack_sum * (1.0 / math.sqrt(day_steps * hosts_here / rack_count))
    pod_drift = pod_sum * (1.0 / math.sqrt(day_steps * hosts_here / POD_DEV))
    return (host_drift, rack_drift, pod_drift)


def solution(mesh):
    in_specs = (P("slab", "hst"), P("hst"), P("hst"))
    out_specs = (P("slab", "hst"), P("slab", "hst"), P("slab", "hst"))
    return jax.shard_map(
        on_device, mesh=mesh, in_specs=in_specs, out_specs=out_specs, check_vma=False
    )
```

profile of v0, /device:TPU:0, one launch (start us, length us, event | category | flops | bytes accessed | tf_op | source)
XLA Modules:
  0.0 104.1 jit_solution(12894285297736445347)
XLA Ops:
  7.2 0.0 all-reduce.4.cloned.1.call-start
  7.2 0.8 add_select_fusion
  8.0 0.0 copy-start.2
  8.0 0.0 copy-start.4
  8.0 0.0 copy-start.1
  8.0 0.0 copy-start.3
  8.0 4.1 %fusion.8 = f32[72,512]{1,0:T(8,128)S(1)} fusion(bf16[72,8192]{1,0:T(8,128)(2,1)} %param.5, s32[8192]{0:T(1024)S(1)} %add_select_fusion), kind=kOutput, calls=%fused_computation.12 | convolution fusion | flops 608174080 | bytes 1359872 | tf_op jit(solution)/shard_map/dot_general | solution.py:77
  12.2 3.0 %collective-permute-start.2 = (f32[72,256]{1,0:T(8,128)S(1)}, f32[72,256]{1,0:T(8,128)S(1)}, u32[]{:S(2)}, u32[]{:S(2)}) collective-permute-start(f32[72,256]{1,0:T(8,128)S(1)} %slice.34), channel_id=1, source_target_pairs={{0,1},{1,2},{2,3},{3,4},{4,5},{5,6},{6,7},{7,0},{8,9},{9,10},{10,1... | collective-permute-start | bytes 221192 | tf_op jit(solution)/shard_map/ppermute | solution.py:26
  15.2 0.0 copy-done.2
  15.2 0.7 collective-permute-start.1
  15.9 0.0 collective-permute-start
  15.9 0.0 copy-done.4
  15.9 0.6 dynamic-slice.1
  17.1 3.4 %collective-permute-done.2 = f32[72,256]{1,0:T(8,128)S(1)} collective-permute-done((f32[72,256]{1,0:T(8,128)S(1)}, f32[72,256]{1,0:T(8,128)S(1)}, u32[]{:S(2)}, u32[]{:S(2)}) %collective-permute-start.2) | collective-permute-done | bytes 73760 | tf_op jit(solution)/shard_map/ppermute | solution.py:26
  20.6 0.0 copy-done.1
  20.6 0.3 fusion.17
  20.8 35.2 %all-reduce.1 = f32[72,16]{1,0:T(8,128)S(1)} all-reduce(f32[72,16]{1,0:T(8,128)S(1)} %fusion.17), channel_id=3, replica_groups=mesh['slab'=4,'hst'=8] {'hst'}, use_global_device_ids=true, to_apply=%region_0.1.clone | all-reduce | flops 1152 | bytes 9216
  56.0 0.1 constant_dynamic-slice_fusion
  56.1 0.1 collective-permute-start.4
  56.2 0.5 collective-permute-start.3
  56.7 0.0 copy-done.3
  56.7 0.6 dynamic-slice
  57.9 0.7 collective-permute-done.4
  58.6 3.0 %collective-permute-done.3 = f32[72,258]{1,0:T(8,128)S(1)} collective-permute-done((f32[72,258]{1,0:T(8,128)S(1)}, f32[72,258]{1,0:T(8,128)S(1)}, u32[]{:S(2)}, u32[]{:S(2)}) %collective-permute-start.3) | collective-permute-done | bytes 74336 | tf_op jit(solution)/shard_map/ppermute | solution.py:36
  61.5 0.3 fusion.9
  61.8 0.2 fusion.23
  62.1 0.0 collective-permute-done.1
  62.1 0.0 collective-permute-done
  62.1 2.1 %fusion.1 = f32[72,8192]{1,0:T(8,128)S(1)} fusion(bf16[72,8192]{1,0:T(8,128)(2,1)S(1)} %collective-permute-done.1, bf16[72,8192]{1,0:T(8,128)(2,1)S(1)} %copy-done.2, bf16[72,8192]{1,0:T(8,128)(2,1)} %collective-permute-done), kind=kOutput, calls=%fused_computation.4 | convolution fusion | flops 267252480 | bytes 5898240 | tf_op jit(solution)/shard_map/dot_general | solution.py:58
  64.3 1.4 %fusion.24 = f32[72,8192]{1,0:T(8,128)S(1)} fusion(f32[72,8192]{1,0:T(8,128)S(1)} %fusion.1), kind=kOutput, calls=%fused_computation.41 | convolution fusion | flops 509613120 | bytes 4718592 | tf_op jit(solution)/shard_map/dot_general | solution.py:60
  65.7 0.2 maximum_dynamic-update-slice_fusion
  65.9 0.0 copy-start
  66.0 0.6 copy-done
  66.6 0.0 all-reduce.4.cloned.1.call-update
  66.6 26.5 %all-reduce.4.cloned.1.call-done = f32[33800]{0:T(1024)} async-done(((f32[33800]{0:T(1024)}), f32[33800]{0:T(1024)}) %all-reduce.4.cloned.1.call-update) | async-done | bytes 135216
  93.2 1.0 %reshape.10 = f32[4,8450]{1,0:T(4,128)S(1)} reshape(f32[33800]{0:T(1024)} %all-reduce.4.cloned.1.call-done) | data formatting | bytes 270400 | tf_op jit(solution)/shard_map/all_gather | solution.py:14
  94.3 0.6 slice_multiply_fusion
  94.9 1.6 %add_multiply_fusion = f32[72,8192]{1,0:T(8,128)} fusion(f32[72,8192]{1,0:T(8,128)S(1)} %fusion.24, f32[8192]{0:T(1024)S(1)} %slice.28), kind=kLoop, calls=%fused_computation.11 | loop fusion | flops 1179648 | bytes 4751360 | tf_op jit(solution)/shard_map/mul | solution.py:119
  96.6 0.6 copy.9
  (12 shorter events, 0.1 us)
Async XLA Ops:
  7.2 86.0 %all-reduce.4.cloned.1.call-start = ((), (), s32[]{:S(2)}) async-start(), calls=%async_computation | async-start | bytes 278528
  8.0 7.2 %copy-start.2 = (bf16[72,8192]{1,0:T(8,128)(2,1)S(1)}, bf16[72,8192]{1,0:T(8,128)(2,1)}, u32[]{:S(2)}) copy-start(bf16[72,8192]{1,0:T(8,128)(2,1)} %param.5) | copy-start | bytes 3538948
  8.0 7.9 %copy-start.4 = (u32[32]{0:T(128)S(1)}, u32[32]{0:T(128)}, u32[]{:S(2)}) copy-start(u32[32]{0:T(128)} %constant.59) | copy-start | bytes 388
  8.0 12.5 %copy-start.1 = (s32[256]{0:T(256)S(1)}, s32[256]{0:T(256)}, u32[]{:S(2)}) copy-start(s32[256]{0:T(256)} %param.7) | copy-start | bytes 3076
  8.0 48.7 %copy-start.3 = (u32[32]{0:T(128)S(1)}, u32[32]{0:T(128)}, u32[]{:S(2)}) copy-start(u32[32]{0:T(128)} %constant.53) | copy-start | bytes 388
  12.2 8.4 %collective-permute-start.2 = (f32[72,256]{1,0:T(8,128)S(1)}, f32[72,256]{1,0:T(8,128)S(1)}, u32[]{:S(2)}, u32[]{:S(2)}) collective-permute-start(f32[72,256]{1,0:T(8,128)S(1)} %slice.34), channel_id=1, source_target_pairs={{0,1},{1,2},{2,3},{3,4},{4,5},{5,6},{6,7},{7,0},{8,9},{9,10},{10,1... | collective-permute-start | bytes 221192 | tf_op jit(solution)/shard_map/ppermute | solution.py:26
  15.2 46.9 %collective-permute-start.1 = (bf16[72,8192]{1,0:T(8,128)(2,1)S(1)}, bf16[72,8192]{1,0:T(8,128)(2,1)S(1)}, u32[]{:S(2)}, u32[]{:S(2)}) collective-permute-start(bf16[72,8192]{1,0:T(8,128)(2,1)S(1)} %copy-done.2), channel_id=1, source_target_pairs={{8,0},{16,8},{24,16},{0,24},{9,1},{17,9},{25,17},{1,25},{10,2},{18... | collective-permute-start | bytes 3538952 | tf_op jit(solution)/shard_map/ppermute | solution.py:38
  15.9 46.2 %collective-permute-start = (bf16[72,8192]{1,0:T(8,128)(2,1)S(1)}, bf16[72,8192]{1,0:T(8,128)(2,1)}, u32[]{:S(2)}, u32[]{:S(2)}) collective-permute-start(bf16[72,8192]{1,0:T(8,128)(2,1)S(1)} %copy-done.2), channel_id=1, source_target_pairs={{0,8},{8,16},{16,24},{24,0},{1,9},{9,17},{17,25},{25,1},{2,10},{10... | collective-permute-start | bytes 3538952 | tf_op jit(solution)/shard_map/ppermute | solution.py:36
  56.1 2.5 %collective-permute-start.4 = (f32[72,258]{1,0:T(8,128)S(1)}, f32[72,258]{1,0:T(8,128)S(1)}, u32[]{:S(2)}, u32[]{:S(2)}) collective-permute-start(f32[72,258]{1,0:T(8,128)S(1)} %pad_maximum_fusion), channel_id=1, source_target_pairs={{8,0},{16,8},{24,16},{0,24},{9,1},{17,9},{25,17},{1,25},{10,2},{18... | collective-permute-start | bytes 222920 | tf_op jit(solution)/shard_map/ppermute | solution.py:38
  56.2 5.4 %collective-permute-start.3 = (f32[72,258]{1,0:T(8,128)S(1)}, f32[72,258]{1,0:T(8,128)S(1)}, u32[]{:S(2)}, u32[]{:S(2)}) collective-permute-start(f32[72,258]{1,0:T(8,128)S(1)} %pad_maximum_fusion), channel_id=1, source_target_pairs={{0,8},{8,16},{16,24},{24,0},{1,9},{9,17},{17,25},{25,1},{2,10},{10... | collective-permute-start | bytes 222920 | tf_op jit(solution)/shard_map/ppermute | solution.py:36
  65.9 0.7 copy-start
Sparse Core Ops, SparseCore 0:
  66.7 26.3 all-reduce.3
where the time goes:
time: 104 us
  blocking collectives  35.2 us (34%)
  waiting for transfers between devices  33.6 us (32%)
  between operations  15.5 us (15%)
  matrix products  8.4 us (8%)
  starting transfers between devices  4.27 us (4%)
  local copies, waits for them, and re-layouts  3.68 us (4%)
  other arithmetic  3.33 us (3%)
    unnamed x1, blocking collectives  35.2 us
    unnamed x2, waiting for transfers between devices  26.6 us
    dot_general x1, matrix products, rack_and_pod(): jnp.dot(series, member, preferred_element_type=jnp.float32, precision=None)  4.12 us
    ppermute x1, waiting for transfers between devices, passed_along(): return lax.ppermute(value, axis, pairs)  3.45 us
    ppermute x1, starting transfers between devices, passed_along(): return lax.ppermute(value, axis, pairs)  2.99 us
    ppermute x2, waiting for transfers between devices, with_halo(): lax.ppermute(tail, axis, [(i, (i + 1) % count) for i in range(count)])  2.97 us
    unnamed x15, local copies, waits for them, and re-layouts  2.57 us
    dot_general x2, matrix products, local_prefix(): jnp.dot(band, extended, preferred_element_type=jnp.float32, precision=pre...  2.43 us
  transfers between devices with their start and end apart: 6, of which 4 were waited for; matrix products, arithmetic and copies ran while one was open for 2% of the time, Pallas kernels for 0%

commit v1 on v0

v1 whole, which is shorter than its diff:
```python
import functools
import math

import jax
import jax.numpy as jnp
from jax import lax
from jax.experimental import pallas as pl
from jax.experimental.pallas import tpu as pltpu
from jax.sharding import PartitionSpec as P

SLAB_LEN = 36
POD_DEV = 2
SLABS = 4
PARTS = 8
MESH = pl.DeviceIdType.MESH
EXACT = lax.Precision.HIGHEST
NT = (((1,), (1,)), ((), ()))


def coefficients(target, source, out_rows, rows):
    reach = 2 * SLAB_LEN
    day = SLABS * rows
    t = target * rows + lax.broadcasted_iota(jnp.int32, (out_rows, rows), 0)
    u = source * rows + lax.broadcasted_iota(jnp.int32, (out_rows, rows), 1)
    value = jnp.where(u <= t, 2 * reach + 1, 0)
    for wrap in (-day, 0, day):
        first = jnp.maximum(u + (wrap - reach), 0)
        last = jnp.minimum(u + (wrap + reach), t)
        value = value - jnp.maximum(last - first + 1, 0)
    return value.astype(jnp.float32)


def kernel(
    shards,
    load_hbm,
    rack_ref,
    pod_ref,
    host_out,
    rack_out,
    pod_out,
    own,
    near,
    far,
    local_rack,
    partial,
    spill,
    totals,
    near_totals,
    far_totals,
    pod_terms,
    pod_in,
    pod_sum,
    slab_pods,
    rack_row,
    rack_row_in,
    host_row,
    host_row_in,
    load_sem,
    near_sems,
    far_send,
    far_recv,
    small_send,
    small_recv,
    pod_send,
    pod_recv,
):
    rows, hosts = own.shape
    racks = totals.shape[1]
    width = hosts // PARTS
    d = lax.axis_index("slab")
    h = lax.axis_index("hst")
    odd = lax.rem(d, 2)
    near_d = d + 1 - 2 * odd
    far_d = lax.rem(d + 3 + 2 * odd, SLABS)
    diag_d = lax.rem(d + 2, SLABS)
    window = 4 * SLAB_LEN + 1
    day = SLABS * rows

    barrier = pltpu.get_barrier_semaphore()
    for peer in (near_d, far_d, diag_d):
        pl.semaphore_signal(barrier, inc=1, device_id=(peer, h), device_id_type=MESH)

    @pl.loop(1, shards)
    def _(k):
        peer = lax.rem(h + k, shards)
        pl.semaphore_signal(barrier, inc=1, device_id=(d, peer), device_id_type=MESH)

    load_copy = pltpu.make_async_copy(load_hbm, own, load_sem)
    load_copy.start()
    local = rack_ref[...] - h * racks
    local_rack[...] = jnp.where(local < 0, local + racks * shards, local)
    pl.semaphore_wait(barrier, SLABS - 1 + shards - 1)

    def far_copy(c):
        cols = pl.ds(pl.multiple_of(c * width, width), width)
        return pltpu.make_async_remote_copy(
            src_ref=load_hbm.at[:, cols],
            dst_ref=far.at[:, cols],
            send_sem=far_send.at[c],
            recv_sem=far_recv.at[c],
            device_id=(far_d, h),
            device_id_type=MESH,
        )

    def small_copy(src, dst, index, device):
        return pltpu.make_async_remote_copy(
            src_ref=src,
            dst_ref=dst,
            send_sem=small_send.at[index],
            recv_sem=small_recv.at[index],
            device_id=device,
            device_id_type=MESH,
        )

    for c in range(PARTS):
        far_copy(c).start()
    near_copy = pltpu.make_async_remote_copy(
        src_ref=load_hbm,
        dst_ref=near,
        send_sem=near_sems.at[0],
        recv_sem=near_sems.at[1],
        device_id=(near_d, h),
        device_id_type=MESH,
    )
    near_copy.start()
    load_copy.wait()

    partial[...] = jnp.zeros_like(partial)
    rack_ids = lax.broadcasted_iota(jnp.int32, (2 * racks, 128), 0)

    @pl.loop(0, PARTS)
    def _(c):
        cols = pl.ds(pl.multiple_of(c * width, width), width)
        member = jnp.concatenate(
            [
                (rack_ids == local_rack[pl.ds(c * (width // 128) + k, 1), :])
                .astype(jnp.float32)
                .astype(jnp.bfloat16)
                for k in range(width // 128)
            ],
            axis=1,
        )
        partial[...] += lax.dot_general(
            own[:, cols], member, NT, preferred_element_type=jnp.float32
        )

    spill_copy = small_copy(
        partial.at[:, pl.ds(racks, racks)], spill, 0, (d, lax.rem(h + 1, shards))
    )
    spill_copy.start()

    k_own = coefficients(d, d, rows, rows)
    k_near = coefficients(d, near_d, rows, rows)
    k_far = coefficients(d, far_d, rows, rows)
    k_diag = coefficients(diag_d, d, 8, rows)
    k_both = jnp.concatenate([k_own, k_diag], 0).astype(jnp.bfloat16)

    @pl.loop(0, PARTS)
    def _(c):
        cols = pl.ds(pl.multiple_of(c * width, width), width)
        both = jnp.dot(k_both, own[:, cols], preferred_element_type=jnp.float32)
        host_out[:, cols] = both[:rows]
        host_row[pl.ds(c, 1), :] = both[rows : rows + 1]

    host_row_copy = small_copy(host_row, host_row_in, 1, (diag_d, h))
    host_row_copy.start()

    spill_copy.wait()
    totals[...] = partial[:, :racks] + spill[...]
    slots = lax.broadcasted_iota(jnp.int32, (8 * shards, 128), 0)
    slot_pod = jnp.where(slots % 8 < POD_DEV, slots // 8 * POD_DEV + slots % 8, -1)
    pod_member = jnp.concatenate(
        [
            (slot_pod == pod_ref[pl.ds(k, 1), :]).astype(jnp.float32)
            for k in range(racks // 128)
        ],
        axis=1,
    )
    pod_terms[...] = lax.dot_general(
        pod_member, totals[...], NT, preferred_element_type=jnp.float32, precision=EXACT
    )

    def pod_copy(k):
        peer = lax.rem(h + k, shards)
        return pltpu.make_async_remote_copy(
            src_ref=pod_terms.at[pl.ds(pl.multiple_of(peer * 8, 8), 8), :],
            dst_ref=pod_in.at[k],
            send_sem=pod_send.at[k],
            recv_sem=pod_recv.at[k],
            device_id=(d, peer),
            device_id_type=MESH,
        )

    @pl.loop(1, shards)
    def _(k):
        pod_copy(k).start()

    rack_row[...] = jnp.dot(
        k_diag, totals[...], preferred_element_type=jnp.float32, precision=EXACT
    )
    copies = [
        small_copy(totals, far_totals, 2, (far_d, h)),
        small_copy(rack_row, rack_row_in, 3, (diag_d, h)),
        small_copy(totals, near_totals, 4, (near_d, h)),
    ]
    for copy in copies:
        copy.start()

    near_copy.wait()
    k_near_half = k_near.astype(jnp.bfloat16)

    @pl.loop(0, PARTS)
    def _(c):
        cols = pl.ds(pl.multiple_of(c * width, width), width)
        host_out[:, cols] += jnp.dot(
            k_near_half, near[:, cols], preferred_element_type=jnp.float32
        )

    pod_sum[...] = pod_terms[pl.ds(pl.multiple_of(h * 8, 8), 8), :]

    @pl.loop(1, shards)
    def _(k):
        pod_copy(k).wait()
        pod_sum[...] += pod_in[k]

    pod_copies = [
        small_copy(pod_sum, slab_pods.at[0], 5, (far_d, h)),
        small_copy(pod_sum, slab_pods.at[1], 6, (diag_d, h)),
        small_copy(pod_sum, slab_pods.at[2], 7, (near_d, h)),
    ]
    for copy in pod_copies:
        copy.start()

    host_row_copy.wait()
    k_far_half = k_far.astype(jnp.bfloat16)
    host_scale = 1.0 / (window * math.sqrt(day))

    def finish(c):
        cols = pl.ds(pl.multiple_of(c * width, width), width)
        far_copy(c).wait()
        host_out[:, cols] = (
            host_out[:, cols]
            + jnp.dot(k_far_half, far[:, cols], preferred_element_type=jnp.float32)
            + host_row_in[pl.ds(c, 1), :]
        ) * host_scale

    @pl.loop(0, PARTS - 2)
    def _(c):
        finish(c)

    for copy in copies + pod_copies:
        copy.wait()

    def exact(a, b):
        return jnp.dot(a, b, preferred_element_type=jnp.float32, precision=EXACT)

    def exact_nt(a, b):
        return lax.dot_general(a, b, NT, preferred_element_type=jnp.float32, precision=EXACT)

    rack_scale = 1.0 / (window * math.sqrt(day * hosts / racks))
    rack_out[...] = (
        exact(k_own, totals[...])
        + exact(k_near, near_totals[...])
        + exact(k_far, far_totals[...])
        + rack_row_in[0:1, :]
    ) * rack_scale
    pod_scale = 1.0 / (window * math.sqrt(day * hosts / POD_DEV))
    pods = (
        exact_nt(pod_sum[...], k_own)
        + exact_nt(slab_pods[0], k_far)
        + exact_nt(slab_pods[1], coefficients(d, diag_d, rows, rows))
        + exact_nt(slab_pods[2], k_near)
    ) * pod_scale
    pod_out[...] = pods[:POD_DEV]

    @pl.loop(PARTS - 2, PARTS)
    def _(c):
        finish(c)


def on_device(load, host_rack, rack_pod):
    rows, hosts = load.shape
    racks = rack_pod.shape[0]
    shards = lax.axis_size("hst")
    f32 = jnp.float32
    vmem = pl.BlockSpec(memory_space=pltpu.VMEM)
    host, rack, pod = pl.pallas_call(
        functools.partial(kernel, shards),
        out_shape=(
            jax.ShapeDtypeStruct((rows, hosts), f32),
            jax.ShapeDtypeStruct((rows, racks), f32),
            jax.ShapeDtypeStruct((POD_DEV, rows), f32),
        ),
        in_specs=[pl.BlockSpec(memory_space=pl.ANY), vmem, vmem],
        out_specs=(vmem, vmem, vmem),
        scratch_shapes=[
            pltpu.VMEM((rows, hosts), load.dtype),
            pltpu.VMEM((rows, hosts), load.dtype),
            pltpu.VMEM((rows, hosts), load.dtype),
            pltpu.VMEM((hosts // 128, 128), jnp.int32),
            pltpu.VMEM((rows, 2 * racks), f32),
            pltpu.VMEM((rows, racks), f32),
            pltpu.VMEM((rows, racks), f32),
            pltpu.VMEM((rows, racks), f32),
            pltpu.VMEM((rows, racks), f32),
            pltpu.VMEM((8 * shards, rows), f32),
            pltpu.VMEM((shards, 8, rows), f32),
            pltpu.VMEM((8, rows), f32),
            pltpu.VMEM((SLABS - 1, 8, rows), f32),
            pltpu.VMEM((8, racks), f32),
            pltpu.VMEM((8, racks), f32),
            pltpu.VMEM((PARTS, hosts // PARTS), f32),
            pltpu.VMEM((PARTS, hosts // PARTS), f32),
            pltpu.SemaphoreType.DMA,
            pltpu.SemaphoreType.DMA((2,)),
            pltpu.SemaphoreType.DMA((PARTS,)),
            pltpu.SemaphoreType.DMA((PARTS,)),
            pltpu.SemaphoreType.DMA((8,)),
            pltpu.SemaphoreType.DMA((8,)),
            pltpu.SemaphoreType.DMA((shards,)),
            pltpu.SemaphoreType.DMA((shards,)),
        ],
        compiler_params=pltpu.CompilerParams(
            collective_id=0, has_side_effects=True, vmem_limit_bytes=40 * 1024 * 1024
        ),
        cost_estimate=pl.CostEstimate(
            flops=2 * rows * hosts * (3 * rows + 2 * racks),
            bytes_accessed=rows * hosts * 10,
            transcendentals=0,
        ),
    )(load, host_rack.reshape(hosts // 128, 128), rack_pod.reshape(racks // 128, 128))
    return host, rack, pod.T


def solution(mesh):
    in_specs = (P("slab", "hst"), P("hst"), P("hst"))
    out_specs = (P("slab", "hst"), P("slab", "hst"), P("slab", "hst"))
    return jax.shard_map(
        on_device, mesh=mesh, in_specs=in_specs, out_specs=out_specs, check_vma=False
    )
```

time: 104 us -> 43.5 us (0.42)
  Pallas kernels: 0 us -> 37.3 us
  blocking collectives: 35.2 us -> 0 us
  waiting for transfers between devices: 33.6 us -> 0 us
  between operations: 15.5 us -> 0.65 us
  matrix products: 8.4 us -> 0 us
  starting transfers between devices: 4.27 us -> 0 us
  other arithmetic: 3.33 us -> 0 us
  local copies, waits for them, and re-layouts: 3.68 us -> 5.3 us
    pallas_call x0 -> x1, Pallas kernels: none -> 37.3 us  [on_device(): pl.pallas_call(functools.partial(kernel, shards), out_shape=(jax.ShapeDty...]
    unnamed x1 -> x0, blocking collectives: 35.2 us -> none
    unnamed x2 -> x0, waiting for transfers between devices: 26.6 us -> none
    dot_general x6 -> x0, matrix products: 8.4 us -> none  [the longest x1 4.12 us: rack_and_pod(): jnp.dot(series, member, preferred_element_type=jnp.float32, precision=None)]
    ppermute x5 -> x0, waiting for transfers between devices: 7.08 us -> none  [the longest x1 3.45 us: passed_along(): return lax.ppermute(value, axis, pairs)]
    ppermute x5 -> x0, starting transfers between devices: 4.23 us -> none  [the longest x1 2.99 us: passed_along(): return lax.ppermute(value, axis, pairs)]
    unnamed x15 -> x9, local copies, waits for them, and re-layouts: 2.57 us -> 5.3 us
    mul x3 -> x0, other arithmetic: 2.29 us -> none  [the longest x1 1.64 us: on_device(): host_drift = host_sum * (1.0 / math.sqrt(day_steps))]
  transfers between devices with their start and end apart: 6 -> 0, of which waited for: 4 -> 0; matrix products, arithmetic and copies ran while one was open for 2% -> 0% of each run, Pallas kernels for 0% -> 0%
where the time goes in v1:
time: 43.5 us; the launch traced here: 43.3 us
  Pallas kernels  37.3 us (86%)
  local copies, waits for them, and re-layouts  5.3 us (12%)
  between operations  0.65 us (1%)
    pallas_call x1, Pallas kernels, on_device(): pl.pallas_call(functools.partial(kernel, shards), out_shape=(jax.ShapeDty...  37.3 us
    unnamed x9, local copies, waits for them, and re-layouts  5.3 us

profile of v1, /device:TPU:0, one launch (start us, length us, event | category | flops | bytes accessed | tf_op | source)
XLA Modules:
  0.0 43.3 jit_solution(12168706118755174788)
XLA Ops:
  0.6 0.0 copy-start
  0.6 1.3 %copy-done = bf16[72,8192]{1,0:T(8,128)(2,1)S(1)} copy-done((bf16[72,8192]{1,0:T(8,128)(2,1)S(1)}, bf16[72,8192]{1,0:T(8,128)(2,1)}, u32[]{:S(2)}) %copy-start) | copy-done | bytes 1179672
  1.9 0.0 copy-start.1
  1.9 0.8 %copy-done.1 = s32[8192]{0:T(1024)S(1)} copy-done((s32[8192]{0:T(1024)S(1)}, s32[8192]{0:T(1024)}, u32[]{:S(2)}) %copy-start.1) | copy-done | bytes 32792
  2.7 0.0 copy-start.2
  2.7 0.7 %copy-done.2 = s32[256]{0:T(256)S(1)} copy-done((s32[256]{0:T(256)S(1)}, s32[256]{0:T(256)}, u32[]{:S(2)}) %copy-start.2) | copy-done | bytes 1048
  3.3 37.3 %shard_map.58 = (f32[72,8192]{1,0:T(8,128)S(1)}, f32[72,256]{1,0:T(8,128)S(1)}, f32[2,72]{1,0:T(2,128)S(1)}) custom-call(bf16[72,8192]{1,0:T(8,128)(2,1)S(1)} %copy-done, s32[64,128]{1,0:T(8,128)S(1)} %bitcast.4, s32[2,128]{1,0:T(2,128)S(1)} %bitcast.5), custom_call_target="tpu_custom_call" | custom-call | flops 858783744 | bytes 5898240 | tf_op jit(solution)/shard_map/pallas_call | solution.py:287
  40.7 1.4 %copy.9 = f32[72,8192]{1,0:T(8,128)} copy(f32[72,8192]{1,0:T(8,128)S(1)} %get-tuple-element.12) | data formatting | bytes 4718592
  42.1 0.6 %copy.10 = f32[72,256]{1,0:T(8,128)} copy(f32[72,256]{1,0:T(8,128)S(1)} %get-tuple-element.13) | data formatting | bytes 147456
  42.7 0.6 %copy.11 = f32[72,2]{0,1:T(2,128)} copy(f32[72,2]{0,1:T(2,128)S(1)} %bitcast.3) | data formatting | bytes 1152
Async XLA Ops:
  0.6 1.3 %copy-start = (bf16[72,8192]{1,0:T(8,128)(2,1)S(1)}, bf16[72,8192]{1,0:T(8,128)(2,1)}, u32[]{:S(2)}) copy-start(bf16[72,8192]{1,0:T(8,128)(2,1)} %load_hbm.1) | copy-start | bytes 3538948
  1.9 0.8 %copy-start.1 = (s32[8192]{0:T(1024)S(1)}, s32[8192]{0:T(1024)}, u32[]{:S(2)}) copy-start(s32[8192]{0:T(1024)} %param.4) | copy-start | bytes 98308
  2.7 0.7 %copy-start.2 = (s32[256]{0:T(256)S(1)}, s32[256]{0:T(256)}, u32[]{:S(2)}) copy-start(s32[256]{0:T(256)} %param.5) | copy-start | bytes 3076
